TPU v7x, 512 devices: a whole 4x8x8 slice. The times are simulated.
512 devices in a mesh: row: 32 (over y_lo, z), col: 16 (over x, y_hi, core).
Axes of the slice: x: 4, y: 8 (y_hi: 2, y_lo: 4; y = y_hi * 4 + y_lo), z: 8, core: 2. Of those that a mesh axis runs over, the one named last changes fastest.
Arguments:
- mask_field: float32 [8192, 2048], P('row', 'col'), may hold values from 0 to 1
- target: int32 [8192, 2048], P('row', 'col'), may hold values 0 or 1
- kernel_real: float32 [4, 128, 128], replicated, may hold values from -0.046875 to 0.046875
- kernel_imag: float32 [4, 128, 128], replicated, may hold values from -0.046875 to 0.046875
Outputs:
- aerial: float32 [8192, 2048], P('row', 'col')
- gradient: float32 [8192, 2048], P('row', 'col')
All inputs are finite; a program needn't handle non-finite values. No bound on the sum of `target` on one device may be relied on, other than what follows from the above.
Results may differ from a plain program's by a relative error of at most 0.00012.
Values sent between devices are 32-bit elements; how exact they have to be, the bound alone decides.
A program may use at most 64 MiB of HBM per device.

v0:
```python
import jax
import jax.numpy as jnp
import numpy as np
from jax import lax
from jax.experimental import pallas as pl
from jax.experimental.pallas import tpu as pltpu
from jax.sharding import PartitionSpec as P

F32, BF16 = jnp.float32, jnp.bfloat16
MESH = pl.DeviceIdType.MESH
steepness = 1.5
threshold = 2.7


def table():
    freq = 2 * np.pi * (np.arange(128) + 0.5) / 256
    col = np.arange(256)
    col = np.where(col < 192, col, col - 256)
    tap = np.arange(128) - 64
    row = np.arange(256)
    both = lambda position, axis: np.concatenate(
        [f(np.outer(position, freq) if axis else np.outer(freq, position)) for f in (np.cos, np.sin)], axis
    )
    back = both(col, 0) * np.repeat([1.0, -1.0], 128)[:, None] / 32768.0
    return np.concatenate([both(tap, 1), both(row, 0), both(col, 1), both(row, 1), back], 0).astype(np.float32)


TABLE = table()
FIRST = 384


def dot(a, b):
    return jnp.dot(a, b, preferred_element_type=F32)


def split(x):
    high = x.astype(BF16)
    return high, (x - high.astype(F32)).astype(BF16)


def lanes(a, b):
    return jnp.concatenate([a, b], axis=1)


def rows(a, b):
    return jnp.concatenate([a, b], axis=0)


def swap(x):
    return pltpu.roll(x, 64, 1)


def butterfly(o):
    cc, cs, sc, ss = o[:128, :128], o[:128, 128:], o[128:, :128], o[128:, 128:]
    return cc - ss, cs + sc, cc + ss, cs - sc


def split_first(tab, t):
    t["wk_hh"][:128], t["wk_l"][...] = split(tab[:128])
    t["wk_hh"][128:] = t["wk_hh"][:128]
    t["cs_h"][...], t["cs_l"][...] = split(tab[128:384])
    t["ca_hh"][:, :128] = t["cs_h"][:, :128]
    t["ca_hh"][:, 128:] = t["cs_h"][:, :128]


def split_second(tab, t):
    t["wm_h"][...], t["wm_l"][...] = split(tab[384:640])
    t["wy_hh"][:128] = t["wm_h"][:128]
    t["wy_hh"][128:] = t["wm_h"][:128]
    t["l2_h"][...], t["l2_l"][...] = split(tab[640:896])
    t["wi_h"][...], t["wi_l"][...] = split(tab[896:1152])
    t["wiy_hl"][:, :128] = t["wi_h"][:, :128]
    t["wiy_hl"][:, 128:] = t["wi_l"][:, :128]


def kernel_spectra(t, k_ref, c_s, H):
    for part in range(2):
        for k in range(4):
            xh, xl = split(k_ref[part, k])
            c = dot(lanes(xh, xl), t["wk_hh"][...]) + dot(xh, t["wk_l"][...])
            c_s[2 * k + part, :128], c_s[2 * k + part, 128:] = split(c)
    for j in range(8):
        o = dot(t["ca_hh"][...], c_s[j]) + dot(t["cs_l"][:, :128], c_s[j, :128])
        for n, v in enumerate(butterfly(o)):
            H[j, n] = v


def mask_spectrum(t, block, M):
    xh, xl = split(block)
    c = dot(xh, t["wm_h"][...]) + dot(xl, t["wm_h"][...]) + dot(xh, t["wm_l"][...])
    ch, cl = split(c)
    o = dot(t["cs_h"][...], ch) + dot(t["cs_h"][...], cl) + dot(t["cs_l"][...], ch)
    for n, v in enumerate(butterfly(o)):
        M[n] = v


def field_rows(t, H, M, d_s, z_s, j):
    def one(n):
        mr, mi, hr, hi = M[n], M[n + 1], H[j, n], H[j, n + 1]
        return mr * hr + mi * hi, mr * hi - mi * hr

    pr, pi = one(0)
    nr, ni = one(2)
    d_s[0, j], d_s[1, j] = split(rows(lanes(pr + nr, pi + ni), lanes(ni - pi, pr - nr)))
    dh, dl = d_s[0, j], d_s[1, j]
    z = dot(t["l2_h"][:128], dh) + dot(t["l2_h"][:128], dl) + dot(t["l2_l"][:128], dh)
    z_s[0, j], z_s[1, j] = split(z)


def field_columns(t, z_s, f, j):
    a = dot(z_s[0, j], t["wiy_hl"][...])
    f[j] = a[:, :128] + a[:, 128:] + dot(z_s[1, j], t["wi_h"][:, :128])


def image(f, target):
    a = f[0] * f[0]
    for j in range(1, 8):
        a = a + f[j] * f[j]
    resist = jax.nn.sigmoid(steepness * (a - threshold))
    return a, 2.0 * (resist - target.astype(F32)) * steepness * resist * (1.0 - resist)


def back_columns(t, f, slope, c_s, j):
    gh, gl = split(slope[...] * f[j])
    c = dot(lanes(gh, gl), t["wy_hh"][...]) + dot(gh, t["wm_l"][:128])
    c_s[j, :128], c_s[j, 128:] = split(c)


def back_rows(t, H, c_s, T, j):
    o = dot(t["ca_hh"][...], c_s[j]) + dot(t["cs_l"][:, :128], c_s[j, :128])
    b = butterfly(o)
    for n in (0, 2):
        gr, gi, hr, hi = b[n], b[n + 1], H[j, n], H[j, n + 1]
        tr, ti = gr * hr - gi * hi, gr * hi + gi * hr
        if j:
            tr, ti = tr + T[n], ti + T[n + 1]
        T[n], T[n + 1] = tr, ti


def final_rows(t, T):
    rp, ip, rm, im = T[0], T[1], T[2], T[3]
    dh, dl = split(2.0 * rows(lanes(rp + rm, -(ip + im)), lanes(ip - im, rp - rm)))
    return split(dot(t["l2_h"][...], dh) + dot(t["l2_h"][...], dl) + dot(t["l2_l"][...], dh))


def final_columns(t, z, which):
    zh, zl = z
    wh, wl = t["wi_h"][:, which], t["wi_l"][:, which]
    return dot(zh, wh) + dot(zl, wh) + dot(zh, wl)


OWN, SIDE = slice(0, 128), slice(128, 256)
SPLITS = dict(
    wk_hh=(256, 256), wk_l=(128, 256), cs_h=(256, 256), cs_l=(256, 256), ca_hh=(256, 256), wm_h=(256, 256),
    wm_l=(256, 256), wy_hh=(256, 256), l2_h=(256, 256), l2_l=(256, 256), wi_h=(256, 256), wi_l=(256, 256),
    wiy_hl=(256, 256),
)


def kernel(mask, target, kr, ki, tab, aerial, gradient,
           E, target_v, k_v, tab_v, H, M, f, slope, T, c_s, d_s, z_s, C, S, aerial_v,
           side_out, side_in, corner_out, corner_in,
           g0_out, g0_in, g1_out, g1_in, gc_out, gc_in, gr_in, local_sem, send_sem, recv_sem, *splits):
    t = dict(zip(SPLITS, splits))
    r, c = lax.axis_index("row"), lax.axis_index("col")
    nr, nc = lax.axis_size("row"), lax.axis_size("col")
    near = {"u": r > 0, "d": r < nr - 1, "l": c > 0, "r": c < nc - 1}
    shift = {"u": (-1, 0), "d": (1, 0), "l": (0, -1), "r": (0, 1)}
    opposite = {"u": "d", "d": "u", "l": "r", "r": "l"}

    def there(way):
        cond = near[way[0]]
        for w in way[1:]:
            cond = jnp.logical_and(cond, near[w])
        return cond

    def device(way):
        return (r + sum(shift[w][0] for w in way), c + sum(shift[w][1] for w in way))

    local = []
    for n, (src, dst) in enumerate(((mask, E.at[0, pl.ds(64, 256)]), (kr, k_v.at[0]), (ki, k_v.at[1]),
                                    (tab.at[pl.ds(0, FIRST)], tab_v.at[pl.ds(0, FIRST)]),
                                    (tab.at[pl.ds(FIRST, 768)], tab_v.at[pl.ds(FIRST, 768)]), (target, target_v))):
        local.append(pltpu.make_async_copy(src, dst, local_sem.at[n]))
        local[-1].start()

    ways = ("l", "r", "u", "d", "ul", "ur", "dl", "dr")
    barrier = pltpu.get_barrier_semaphore()
    for way in ways:
        @pl.when(there(way))
        def _():
            pl.semaphore_signal(barrier, inc=1, device_id=device(way), device_id_type=MESH)

    def empty(way, *refs):
        @pl.when(jnp.logical_not(there(way)))
        def _():
            for ref in refs:
                ref[...] = jnp.zeros(ref.shape, F32)

    place = {"l": 0, "r": 1}
    for way in "lr":
        n = 1 - place[way]
        empty(way, side_in.at[:, n], g0_in.at[n], g1_in.at[n])
        empty("u" + way, corner_in.at[0, n], gc_in.at[0, n])
        empty("d" + way, corner_in.at[1, n], gc_in.at[1, n])
    empty("u", E.at[0, pl.ds(0, 64)], gr_in.at[0])
    empty("d", E.at[0, pl.ds(320, 64)], gr_in.at[1])

    sent = []

    def message(way, src, dst):
        n = len(sent)
        copy = pltpu.make_async_remote_copy(src_ref=src, dst_ref=dst, send_sem=send_sem.at[n], recv_sem=recv_sem.at[n],
                                            device_id=device(way), device_id_type=MESH)
        sent.append((copy, way))

        @pl.when(there(way))
        def _():
            copy.start()

        return copy, "".join(opposite[w] for w in way)

    def arrive(*messages):
        for copy, come in messages:
            @pl.when(there(come))
            def _(copy=copy):
                copy.wait_recv()

    def is_low(n):
        return lax.broadcasted_iota(jnp.int32, (n, 128), 1) < 64

    def pack(ref, first, second, low_place=0):
        low, second = is_low(first.shape[0]), swap(second)
        ref[low_place] = jnp.where(low, first, second)
        ref[1 - low_place] = jnp.where(low, second, first)

    local[0].wait()
    for k in range(2):
        pack(side_out.at[k], E[0, 64 + 128 * k : 128 + 128 * k], E[0, 128 + 128 * k : 192 + 128 * k])
    pack(corner_out.at[0], E[0, 256:288], E[0, 288:320])
    pack(corner_out.at[1], E[0, 64:96], E[0, 96:128])
    pl.semaphore_wait(barrier, sum(there(way).astype(jnp.int32) for way in ways))
    sides = [[message(way, side_out.at[0, place[way]], side_in.at[0, place[way]]) for way in "lr"]]
    above = [message("d" + way, corner_out.at[0, place[way]], corner_in.at[0, place[way]]) for way in "lr"]
    sides.append([message(way, side_out.at[1, place[way]], side_in.at[1, place[way]]) for way in "lr"])
    above.append(message("d", E.at[0, pl.ds(256, 64)], E.at[0, pl.ds(0, 64)]))
    below = [message("u" + way, corner_out.at[1, place[way]], corner_in.at[1, place[way]]) for way in "lr"]
    below.append(message("u", E.at[0, pl.ds(64, 64)], E.at[0, pl.ds(320, 64)]))

    local[3].wait()
    split_first(tab_v, t)
    local[1].wait()
    local[2].wait()
    kernel_spectra(t, k_v, c_s.at[0], H)
    local[4].wait()
    split_second(tab_v, t)
    local[5].wait()

    def unpack(ref, start):
        n = ref.shape[1]
        low, from_right, from_left = is_low(n), ref[0], ref[1]
        E[1, start : start + n] = jnp.where(low, from_right, from_left)
        E[1, start + n : start + 2 * n] = swap(jnp.where(low, from_left, from_right))

    arrive(*sides[0], *sides[1], *above)
    unpack(side_in.at[0], 64)
    unpack(side_in.at[1], 192)
    unpack(corner_in.at[0], 0)
    mask_spectrum(t, lanes(E[0, :256], E[1, :256]), M.at[0])
    for j in range(8):
        field_rows(t, H, M.at[0], d_s.at[0], z_s.at[0], j)
    for j in range(8):
        field_columns(t, z_s.at[0], f.at[0], j)
    aerial_v[:128], slope[0] = image(f.at[0], target_v[:128])
    arrive(*below)
    unpack(corner_in.at[1], 320)
    mask_spectrum(t, lanes(E[0, 128:], E[1, 128:]), M.at[1])
    for j in range(8):
        back_columns(t, f.at[0], slope.at[0], c_s.at[1], j)
        field_rows(t, H, M.at[1], d_s.at[1], z_s.at[1], j)
    for j in range(8):
        back_rows(t, H, c_s.at[1], T.at[0], j)
        field_columns(t, z_s.at[1], f.at[1], j)
    aerial_v[128:], slope[1] = image(f.at[1], target_v[128:])
    aerial_out = pltpu.make_async_copy(aerial_v, aerial, local_sem.at[6])
    aerial_out.start()
    z = final_rows(t, T.at[0])
    S[0] = final_columns(t, z, SIDE)
    pack(gc_out.at[0], S[0, 0:32], S[0, 32:64], 1)
    pack(g0_out, S[0, 64:96], S[0, 96:128], 1)
    C[0] = final_columns(t, z, OWN)
    early = [message("u" + way, gc_out.at[0, place[way]], gc_in.at[1, place[way]]) for way in "lr"]
    early += [message(way, g0_out.at[place[way]], g0_in.at[place[way]]) for way in "lr"]
    early.append(message("u", C.at[0, pl.ds(0, 64)], gr_in.at[1]))
    for j in range(8):
        back_columns(t, f.at[1], slope.at[1], c_s.at[2], j)
    for j in range(8):
        back_rows(t, H, c_s.at[2], T.at[1], j)
    z = final_rows(t, T.at[1])
    S[1] = final_columns(t, z, SIDE)
    middle = S[0, 128:256] + S[1, 0:128]
    pack(g1_out, middle[:96], rows(middle[96:], S[1, 128:192]), 1)
    pack(gc_out.at[1], S[1, 192:224], S[1, 224:256], 1)
    late = [message(way, g1_out.at[place[way]], g1_in.at[place[way]]) for way in "lr"]
    late += [message("d" + way, gc_out.at[1, place[way]], gc_in.at[0, place[way]]) for way in "lr"]
    C[1] = final_columns(t, z, OWN)
    late.append(message("d", C.at[1, pl.ds(192, 64)], gr_in.at[0]))
    own = rows(C[0, 64:256], C[1, 128:192])
    own = rows(own[:64], rows(own[64:192] + C[1, 0:128], own[192:]))

    def gain(ref):
        low, from_right, from_left = is_low(ref.shape[1]), ref[0], ref[1]
        return rows(jnp.where(low, from_left, from_right), swap(jnp.where(low, from_right, from_left)))

    arrive(*early)
    arrive(*late)
    add = rows(gain(g0_in), gain(g1_in))
    add = rows(add[:64] + gain(gc_in.at[0]) + gr_in[0], rows(add[64:192], add[192:] + gain(gc_in.at[1]) + gr_in[1]))
    S[0, :256] = own + add
    gradient_out = pltpu.make_async_copy(S.at[0], gradient, local_sem.at[7])
    gradient_out.start()
    for copy, way in sent:
        @pl.when(there(way))
        def _():
            copy.wait_send()
    aerial_out.wait()
    gradient_out.wait()


def hand_over(first, second, first_out, second_out, buf, sem):
    ins = [pltpu.make_async_copy(src, buf.at[n], sem.at[n]) for n, src in enumerate((first, second))]
    outs = [pltpu.make_async_copy(buf.at[n], dst, sem.at[2 + n]) for n, dst in enumerate((first_out, second_out))]
    for copy in ins:
        copy.start()
    for copy, out in zip(ins, outs):
        copy.wait()
        out.start()
    for out in outs:
        out.wait()


def local(mask_field, target, kernel_real, kernel_imag):
    V, HBM = pltpu.VMEM, pltpu.HBM
    tile = jax.ShapeDtypeStruct(mask_field.shape, F32)
    results = pl.pallas_call(
        kernel,
        out_shape=(tile, tile),
        in_specs=[pl.BlockSpec(memory_space=HBM)] * 5,
        out_specs=[pl.BlockSpec(memory_space=HBM)] * 2,
        scratch_shapes=[
            V((2, 384, 128), F32),
            V((256, 128), jnp.int32),
            V((2, 4, 128, 128), F32),
            V(TABLE.shape, F32),
            V((8, 4, 128, 128), F32),
            V((2, 4, 128, 128), F32),
            V((2, 8, 128, 128), F32),
            V((2, 128, 128), F32),
            V((2, 4, 128, 128), F32),
            V((3, 8, 256, 256), BF16),
            V((2, 2, 8, 256, 256), BF16),
            V((2, 2, 8, 128, 256), BF16),
            V((2, 256, 128), F32),
            V((2, 256, 128), F32),
            V((256, 128), F32),
            V((2, 2, 64, 128), F32),
            V((2, 2, 64, 128), F32),
            V((2, 2, 32, 128), F32),
            V((2, 2, 32, 128), F32),
            V((2, 32, 128), F32),
            V((2, 32, 128), F32),
            V((2, 96, 128), F32),
            V((2, 96, 128), F32),
            V((2, 2, 32, 128), F32),
            V((2, 2, 32, 128), F32),
            V((2, 64, 128), F32),
            pltpu.SemaphoreType.DMA((8,)),
            pltpu.SemaphoreType.DMA((20,)),
            pltpu.SemaphoreType.DMA((20,)),
        ] + [V(shape, BF16) for shape in SPLITS.values()],
        compiler_params=pltpu.CompilerParams(vmem_limit_bytes=60 * 2**20, collective_id=0, has_side_effects=True),
        name="litho",
    )(mask_field, target, kernel_real, kernel_imag, jnp.asarray(TABLE))
    return pl.pallas_call(
        hand_over,
        out_shape=(tile, tile),
        in_specs=[pl.BlockSpec(memory_space=HBM)] * 2,
        out_specs=[pl.BlockSpec(memory_space=HBM)] * 2,
        scratch_shapes=[V((2, 256, 128), F32), pltpu.SemaphoreType.DMA((4,))],
        name="hand_over",
    )(*results)


def solution(mesh):
    in_specs = (P("row", "col"), P("row", "col"), P(), P())
    out_specs = (P("row", "col"), P("row", "col"))
    return jax.shard_map(local, mesh=mesh, in_specs=in_specs, out_specs=out_specs, check_vma=False)
```

profile of v0, /device:TPU:13, one launch (start us, length us, event | category | flops | bytes accessed | tf_op | source)
XLA Modules:
  0.0 40.3 jit_solution(191391052595647222)
XLA Ops:
  0.6 38.0 %litho.1 = (f32[256,128]{1,0:T(8,128)}, f32[256,128]{1,0:T(8,128)}) custom-call(f32[256,128]{1,0:T(8,128)} %mask.1, s32[256,128]{1,0:T(8,128)} %target.1, f32[4,128,128]{2,1,0:T(8,128)} %kr.1, f32[4,128,128]{2,1,0:T(8,128)} %ki.1, f32[1152,256]{1,0:T(8,128)} %constant.2.clone.tab), custom_call_target="tpu_custom_call" | custom-call | tf_op jit(solution)/shard_map/litho/pallas_call | solution.py:345
  38.6 1.7 %hand_over.1 = (f32[256,128]{1,0:T(8,128)}, f32[256,128]{1,0:T(8,128)}) custom-call(f32[256,128]{1,0:T(8,128)} %get-tuple-element.4.first, f32[256,128]{1,0:T(8,128)} %get-tuple-element.5.second), custom_call_target="tpu_custom_call" | custom-call | tf_op jit(solution)/shard_map/hand_over/pallas_call | solution.py:384
where the time goes:
time: 40.4 us; the launch traced here: 40.3 us
  Pallas kernels  39.6 us (98%)
  between operations  0.64 us (2%)
    pallas_call x1, Pallas kernels, local(): pl.pallas_call(kernel, out_shape=(tile, tile), in_specs=[pl.BlockSpec(mem...  38 us
    pallas_call x1, Pallas kernels, local(): pl.pallas_call(hand_over, out_shape=(tile, tile), in_specs=[pl.BlockSpec(...  1.66 us

commit v1 on v0

--- a/solution.py
+++ b/solution.py
@@ -158,9 +158,9 @@
 
 
 def kernel(mask, target, kr, ki, tab, aerial, gradient,
-           E, target_v, k_v, tab_v, H, M, f, slope, T, c_s, d_s, z_s, C, S, aerial_v,
+           E, target_v, k_v, tab_v, H, M, f, slope, T, c_s, d_s, z_s, C, S, aerial_v, grad_v,
            side_out, side_in, corner_out, corner_in,
-           g0_out, g0_in, g1_out, g1_in, gc_out, gc_in, gr_in, local_sem, send_sem, recv_sem, *splits):
+           g0_out, g0_in, g1_out, g1_in, gc_out, gc_in, gr_in, local_sem, send_sem, recv_sem, ready, *splits):
     t = dict(zip(SPLITS, splits))
     r, c = lax.axis_index("row"), lax.axis_index("col")
     nr, nc = lax.axis_size("row"), lax.axis_size("col")
@@ -186,8 +186,11 @@
 
     ways = ("l", "r", "u", "d", "ul", "ur", "dl", "dr")
     barrier = pltpu.get_barrier_semaphore()
+    z = lax.rem(r, 8)
+    opens, closes = z == 0, z == 7
     for way in ways:
-        @pl.when(there(way))
+        tells = jnp.logical_and(there(way), jnp.logical_not(closes)) if way[0] == "d" else there(way)
+        @pl.when(tells)
         def _():
             pl.semaphore_signal(barrier, inc=1, device_id=device(way), device_id_type=MESH)
 
@@ -206,6 +209,11 @@
     empty("u", E.at[0, pl.ds(0, 64)], gr_in.at[0])
     empty("d", E.at[0, pl.ds(320, 64)], gr_in.at[1])
 
+    lower = jnp.logical_or(opens, closes)
+    upper = jnp.logical_not(lower)
+    first = lower.astype(jnp.int32)
+    second = 1 - first
+
     sent = []
 
     def message(way, src, dst):
@@ -213,16 +221,19 @@
         copy = pltpu.make_async_remote_copy(src_ref=src, dst_ref=dst, send_sem=send_sem.at[n], recv_sem=recv_sem.at[n],
                                             device_id=device(way), device_id_type=MESH)
         sent.append((copy, way))
-
-        @pl.when(there(way))
-        def _():
-            copy.start()
-
-        return copy, "".join(opposite[w] for w in way)
-
-    def arrive(*messages):
-        for copy, come in messages:
-            @pl.when(there(come))
+        return copy, way
+
+    def start(messages, now=None):
+        for copy, way in messages:
+            go = there(way)
+            @pl.when(go if now is None else jnp.logical_and(go, now))
+            def _(copy=copy):
+                copy.start()
+
+    def arrive(messages, now=None):
+        for copy, way in messages:
+            come = there("".join(opposite[w] for w in way))
+            @pl.when(come if now is None else jnp.logical_and(come, now))
             def _(copy=copy):
                 copy.wait_recv()
 
@@ -233,19 +244,36 @@
         low, second = is_low(first.shape[0]), swap(second)
         ref[low_place] = jnp.where(low, first, second)
         ref[1 - low_place] = jnp.where(low, second, first)
+
+    def both(src, dst, toward=""):
+        return [message(toward + way, src.at[place[way]], dst.at[place[way]]) for way in "lr"]
+
+    side = [both(side_out.at[k], side_in.at[k]) for k in range(2)]
+    to_below = both(corner_out.at[0], corner_in.at[0], "d") + [
+        message("d", E.at[0, pl.ds(256, 64)], E.at[0, pl.ds(0, 64)])]
+    to_above = both(corner_out.at[1], corner_in.at[1], "u") + [
+        message("u", E.at[0, pl.ds(64, 64)], E.at[0, pl.ds(320, 64)])]
+    out_above = both(gc_out.at[0], gc_in.at[1], "u") + [message("u", C.at[first, pl.ds(0, 64)], gr_in.at[1])]
+    out_below = both(gc_out.at[1], gc_in.at[0], "d") + [message("d", C.at[second, pl.ds(192, 64)], gr_in.at[0])]
+    out_edge = both(g0_out, g0_in)
+    out_rest = both(g1_out, g1_in)
 
     local[0].wait()
     for k in range(2):
         pack(side_out.at[k], E[0, 64 + 128 * k : 128 + 128 * k], E[0, 128 + 128 * k : 192 + 128 * k])
     pack(corner_out.at[0], E[0, 256:288], E[0, 288:320])
     pack(corner_out.at[1], E[0, 64:96], E[0, 96:128])
-    pl.semaphore_wait(barrier, sum(there(way).astype(jnp.int32) for way in ways))
-    sides = [[message(way, side_out.at[0, place[way]], side_in.at[0, place[way]]) for way in "lr"]]
-    above = [message("d" + way, corner_out.at[0, place[way]], corner_in.at[0, place[way]]) for way in "lr"]
-    sides.append([message(way, side_out.at[1, place[way]], side_in.at[1, place[way]]) for way in "lr"])
-    above.append(message("d", E.at[0, pl.ds(256, 64)], E.at[0, pl.ds(0, 64)]))
-    below = [message("u" + way, corner_out.at[1, place[way]], corner_in.at[1, place[way]]) for way in "lr"]
-    below.append(message("u", E.at[0, pl.ds(64, 64)], E.at[0, pl.ds(320, 64)]))
+    def heard(way):
+        return jnp.logical_and(there(way), jnp.logical_not(opens)) if way[0] == "u" else there(way)
+
+    pl.semaphore_wait(barrier, sum(heard(way).astype(jnp.int32) for way in ways))
+    for k, way in enumerate(("d", "dl", "dr")):
+        @pl.when(jnp.logical_and(there(way), closes))
+        def _():
+            pl.semaphore_signal(ready.at[k], inc=1, device_id=device(way), device_id_type=MESH)
+
+    start(side[0] + side[1] + to_below)
+    start(to_above, jnp.logical_not(opens))
 
     local[3].wait()
     split_first(tab_v, t)
@@ -256,68 +284,102 @@
     split_second(tab_v, t)
     local[5].wait()
 
-    def unpack(ref, start):
+    def unpack(ref, begin):
         n = ref.shape[1]
         low, from_right, from_left = is_low(n), ref[0], ref[1]
-        E[1, start : start + n] = jnp.where(low, from_right, from_left)
-        E[1, start + n : start + 2 * n] = swap(jnp.where(low, from_left, from_right))
-
-    arrive(*sides[0], *sides[1], *above)
+        E[1, pl.ds(begin, n)] = jnp.where(low, from_right, from_left)
+        E[1, pl.ds(begin + n, n)] = swap(jnp.where(low, from_left, from_right))
+
+    def spectrum(n, b):
+        unpack(corner_in.at[b], pl.multiple_of(320 * b, 64))
+        span = pl.ds(pl.multiple_of(128 * b, 128), 256)
+        mask_spectrum(t, lanes(E[0, span], E[1, span]), M.at[n])
+
+    def expose(n, b):
+        span = pl.ds(pl.multiple_of(128 * b, 128), 128)
+        aerial_v[span], slope[n] = image(f.at[n], target_v[span])
+
+    def outer(b):
+        return pl.multiple_of(192 * b, 64)
+
+    def edge(b):
+        return pl.multiple_of(64 + 64 * b, 64)
+
+    def pack_outer(n, b):
+        start_row = outer(b)
+        pack(gc_out.at[b], S[n, pl.ds(start_row, 32)], S[n, pl.ds(start_row + 32, 32)], 1)
+
+    for odd in (1, 0):
+        for (copy, way), k in zip(to_above, (2, 1, 0)):
+            column = c + sum(shift[w][1] for w in way)
+            @pl.when(jnp.logical_and(jnp.logical_and(there(way), opens), lax.rem(lax.div(column, 2), 2) == odd))
+            def _(copy=copy, k=k):
+                pl.semaphore_wait(ready.at[k], 1)
+                copy.start()
+
+    arrive(side[0] + side[1])
+    arrive(to_below, upper)
+    arrive(to_above, lower)
     unpack(side_in.at[0], 64)
     unpack(side_in.at[1], 192)
-    unpack(corner_in.at[0], 0)
-    mask_spectrum(t, lanes(E[0, :256], E[1, :256]), M.at[0])
+    spectrum(0, first)
     for j in range(8):
         field_rows(t, H, M.at[0], d_s.at[0], z_s.at[0], j)
     for j in range(8):
         field_columns(t, z_s.at[0], f.at[0], j)
-    aerial_v[:128], slope[0] = image(f.at[0], target_v[:128])
-    arrive(*below)
-    unpack(corner_in.at[1], 320)
-    mask_spectrum(t, lanes(E[0, 128:], E[1, 128:]), M.at[1])
+    expose(0, first)
     for j in range(8):
         back_columns(t, f.at[0], slope.at[0], c_s.at[1], j)
+    for j in range(8):
+        back_rows(t, H, c_s.at[1], T.at[0], j)
+    zz = final_rows(t, T.at[0])
+    S[0] = final_columns(t, zz, SIDE)
+    pack_outer(0, first)
+    edge_row = edge(first)
+    pack(g0_out, S[0, pl.ds(edge_row, 32)], S[0, pl.ds(edge_row + 32, 32)], 1)
+    C[0] = final_columns(t, zz, OWN)
+    start(out_above, upper)
+    start(out_below, lower)
+    start(out_edge)
+    arrive(to_below, lower)
+    arrive(to_above, upper)
+    spectrum(1, second)
+    for j in range(8):
         field_rows(t, H, M.at[1], d_s.at[1], z_s.at[1], j)
     for j in range(8):
-        back_rows(t, H, c_s.at[1], T.at[0], j)
         field_columns(t, z_s.at[1], f.at[1], j)
-    aerial_v[128:], slope[1] = image(f.at[1], target_v[128:])
+    expose(1, second)
     aerial_out = pltpu.make_async_copy(aerial_v, aerial, local_sem.at[6])
     aerial_out.start()
-    z = final_rows(t, T.at[0])
-    S[0] = final_columns(t, z, SIDE)
-    pack(gc_out.at[0], S[0, 0:32], S[0, 32:64], 1)
-    pack(g0_out, S[0, 64:96], S[0, 96:128], 1)
-    C[0] = final_columns(t, z, OWN)
-    early = [message("u" + way, gc_out.at[0, place[way]], gc_in.at[1, place[way]]) for way in "lr"]
-    early += [message(way, g0_out.at[place[way]], g0_in.at[place[way]]) for way in "lr"]
-    early.append(message("u", C.at[0, pl.ds(0, 64)], gr_in.at[1]))
     for j in range(8):
         back_columns(t, f.at[1], slope.at[1], c_s.at[2], j)
     for j in range(8):
         back_rows(t, H, c_s.at[2], T.at[1], j)
-    z = final_rows(t, T.at[1])
-    S[1] = final_columns(t, z, SIDE)
-    middle = S[0, 128:256] + S[1, 0:128]
-    pack(g1_out, middle[:96], rows(middle[96:], S[1, 128:192]), 1)
-    pack(gc_out.at[1], S[1, 192:224], S[1, 224:256], 1)
-    late = [message(way, g1_out.at[place[way]], g1_in.at[place[way]]) for way in "lr"]
-    late += [message("d" + way, gc_out.at[1, place[way]], gc_in.at[0, place[way]]) for way in "lr"]
-    C[1] = final_columns(t, z, OWN)
-    late.append(message("d", C.at[1, pl.ds(192, 64)], gr_in.at[0]))
-    own = rows(C[0, 64:256], C[1, 128:192])
-    own = rows(own[:64], rows(own[64:192] + C[1, 0:128], own[192:]))
+    zz = final_rows(t, T.at[1])
+    S[1] = final_columns(t, zz, SIDE)
+    pack_outer(1, second)
+    middle = S[first, 128:256] + S[second, 0:128]
+    pack(g1_out, middle[:96], rows(middle[96:], S[1, pl.ds(edge(second), 64)]), 1)
+    C[1] = final_columns(t, zz, OWN)
+    start(out_rest)
+    start(out_above, lower)
+    start(out_below, upper)
+    grad_v[:64] = C[first, 64:128]
+    grad_v[64:192] = C[first, 128:256] + C[second, 0:128]
+    grad_v[192:] = C[second, 128:192]
 
     def gain(ref):
         low, from_right, from_left = is_low(ref.shape[1]), ref[0], ref[1]
         return rows(jnp.where(low, from_left, from_right), swap(jnp.where(low, from_right, from_left)))
 
-    arrive(*early)
-    arrive(*late)
-    add = rows(gain(g0_in), gain(g1_in))
-    add = rows(add[:64] + gain(gc_in.at[0]) + gr_in[0], rows(add[64:192], add[192:] + gain(gc_in.at[1]) + gr_in[1]))
-    S[0, :256] = own + add
-    gradient_out = pltpu.make_async_copy(S.at[0], gradient, local_sem.at[7])
+    arrive(out_edge + out_rest + out_above + out_below)
+    rest = gain(g1_in)
+    grad_v[64:192] += rest[:128]
+    grad_v[pl.ds(pl.multiple_of(192 * second, 64), 64)] += rest[128:]
+    grad_v[pl.ds(pl.multiple_of(192 * first, 64), 64)] += gain(g0_in)
+    grad_v[:64] += gain(gc_in.at[0]) + gr_in[0]
+    grad_v[192:] += gain(gc_in.at[1]) + gr_in[1]
+    gradient_out = pltpu.make_async_copy(grad_v, gradient, local_sem.at[7])
     gradient_out.start()
     for copy, way in sent:
         @pl.when(there(way))
@@ -363,6 +425,7 @@
             V((2, 256, 128), F32),
             V((2, 256, 128), F32),
             V((256, 128), F32),
+            V((256, 128), F32),
             V((2, 2, 64, 128), F32),
             V((2, 2, 64, 128), F32),
             V((2, 2, 32, 128), F32),
@@ -377,6 +440,7 @@
             pltpu.SemaphoreType.DMA((8,)),
             pltpu.SemaphoreType.DMA((20,)),
             pltpu.SemaphoreType.DMA((20,)),
+            pltpu.SemaphoreType.REGULAR((3,)),
         ] + [V(shape, BF16) for shape in SPLITS.values()],
         compiler_params=pltpu.CompilerParams(vmem_limit_bytes=60 * 2**20, collective_id=0, has_side_effects=True),
         name="litho",

time: 40.4 us -> 36.4 us (0.901)
  the two profiles are of different devices: /device:TPU:13 before, /device:TPU:12 now
where the time goes in v1:
time: 36.4 us; the launch traced here: 36.2 us
  Pallas kernels  35.6 us (98%)
  between operations  0.64 us (2%)
    pallas_call x1, Pallas kernels, local(): pl.pallas_call(kernel, out_shape=(tile, tile), in_specs=[pl.BlockSpec(mem...  33.9 us
    pallas_call x1, Pallas kernels, local(): pl.pallas_call(hand_over, out_shape=(tile, tile), in_specs=[pl.BlockSpec(...  1.66 us

profile of v1, /device:TPU:12, one launch (start us, length us, event | category | flops | bytes accessed | tf_op | source)
XLA Modules:
  0.0 36.2 jit_solution(2288849110819770783)
XLA Ops:
  0.6 33.9 %litho.1 = (f32[256,128]{1,0:T(8,128)}, f32[256,128]{1,0:T(8,128)}) custom-call(f32[256,128]{1,0:T(8,128)} %mask.1, s32[256,128]{1,0:T(8,128)} %target.1, f32[4,128,128]{2,1,0:T(8,128)} %kr.1, f32[4,128,128]{2,1,0:T(8,128)} %ki.1, f32[1152,256]{1,0:T(8,128)} %constant.2.clone.tab), custom_call_target="tpu_custom_call" | custom-call | tf_op jit(solution)/shard_map/litho/pallas_call | solution.py:407
  34.5 1.7 %hand_over.1 = (f32[256,128]{1,0:T(8,128)}, f32[256,128]{1,0:T(8,128)}) custom-call(f32[256,128]{1,0:T(8,128)} %get-tuple-element.4.first, f32[256,128]{1,0:T(8,128)} %get-tuple-element.5.second), custom_call_target="tpu_custom_call" | custom-call | tf_op jit(solution)/shard_map/hand_over/pallas_call | solution.py:448

commit v2 on v1

--- a/solution.py
+++ b/solution.py
@@ -157,10 +157,15 @@
 )
 
 
-def kernel(mask, target, kr, ki, tab, aerial, gradient,
+def lower_first(r):
+    z = lax.rem(r, 8)
+    return jnp.logical_or(z == 0, z == 7)
+
+
+def kernel(mask, target, kr, ki, tab, aerial, partial, g0_in, g1_in, gc_in, gr_in,
            E, target_v, k_v, tab_v, H, M, f, slope, T, c_s, d_s, z_s, C, S, aerial_v, grad_v,
-           side_out, side_in, corner_out, corner_in,
-           g0_out, g0_in, g1_out, g1_in, gc_out, gc_in, gr_in, local_sem, send_sem, recv_sem, ready, *splits):
+           side_out, side_in, edge_in, corner_out, corner_in,
+           g0_out, g1_out, gc_out, local_sem, send_sem, recv_sem, ready, *splits):
     t = dict(zip(SPLITS, splits))
     r, c = lax.axis_index("row"), lax.axis_index("col")
     nr, nc = lax.axis_size("row"), lax.axis_size("col")
@@ -188,11 +193,27 @@
     barrier = pltpu.get_barrier_semaphore()
     z = lax.rem(r, 8)
     opens, closes = z == 0, z == 7
-    for way in ways:
-        tells = jnp.logical_and(there(way), jnp.logical_not(closes)) if way[0] == "d" else there(way)
-        @pl.when(tells)
+    inner_up, inner_down = jnp.logical_and(near["u"], jnp.logical_not(opens)), jnp.logical_and(near["d"], jnp.logical_not(closes))
+    ways = ("l", "r", "u", "d", "ul", "ur", "dl", "dr")
+    tells = {"l": near["l"], "r": near["r"], "u": near["u"], "d": inner_down,
+             "ul": jnp.logical_and(opens, there("ul")), "ur": jnp.logical_and(opens, there("ur"))}
+    hears = {"l": near["l"], "r": near["r"], "u": inner_up, "d": near["d"],
+             "dl": jnp.logical_and(closes, there("dl")), "dr": jnp.logical_and(closes, there("dr"))}
+    barrier = pltpu.get_barrier_semaphore()
+    for way, cond in tells.items():
+        @pl.when(cond)
         def _():
             pl.semaphore_signal(barrier, inc=1, device_id=device(way), device_id_type=MESH)
+
+    def word(sem, way, cond):
+        @pl.when(cond)
+        def _():
+            pl.semaphore_signal(sem, inc=1, device_id=device(way), device_id_type=MESH)
+
+    def hear(sem, cond):
+        @pl.when(cond)
+        def _():
+            pl.semaphore_wait(sem, 1)
 
     def empty(way, *refs):
         @pl.when(jnp.logical_not(there(way)))
@@ -203,13 +224,13 @@
     place = {"l": 0, "r": 1}
     for way in "lr":
         n = 1 - place[way]
-        empty(way, side_in.at[:, n], g0_in.at[n], g1_in.at[n])
-        empty("u" + way, corner_in.at[0, n], gc_in.at[0, n])
-        empty("d" + way, corner_in.at[1, n], gc_in.at[1, n])
-    empty("u", E.at[0, pl.ds(0, 64)], gr_in.at[0])
-    empty("d", E.at[0, pl.ds(320, 64)], gr_in.at[1])
-
-    lower = jnp.logical_or(opens, closes)
+        empty(way, side_in.at[n], edge_in.at[:, n])
+        empty("u" + way, corner_in.at[0, n])
+        empty("d" + way, corner_in.at[1, n])
+    empty("u", E.at[0, pl.ds(0, 64)])
+    empty("d", E.at[0, pl.ds(320, 64)])
+
+    lower = lower_first(r)
     upper = jnp.logical_not(lower)
     first = lower.astype(jnp.int32)
     second = 1 - first
@@ -248,38 +269,43 @@
     def both(src, dst, toward=""):
         return [message(toward + way, src.at[place[way]], dst.at[place[way]]) for way in "lr"]
 
-    side = [both(side_out.at[k], side_in.at[k]) for k in range(2)]
+    side = both(side_out, side_in)
+    edges = [both(corner_out.at[1 - k], edge_in.at[k]) for k in range(2)]
     to_below = both(corner_out.at[0], corner_in.at[0], "d") + [
         message("d", E.at[0, pl.ds(256, 64)], E.at[0, pl.ds(0, 64)])]
     to_above = both(corner_out.at[1], corner_in.at[1], "u") + [
         message("u", E.at[0, pl.ds(64, 64)], E.at[0, pl.ds(320, 64)])]
-    out_above = both(gc_out.at[0], gc_in.at[1], "u") + [message("u", C.at[first, pl.ds(0, 64)], gr_in.at[1])]
-    out_below = both(gc_out.at[1], gc_in.at[0], "d") + [message("d", C.at[second, pl.ds(192, 64)], gr_in.at[0])]
+    corner_above, row_above = both(gc_out.at[0], gc_in.at[1], "u"), [message("u", C.at[first, pl.ds(0, 64)], gr_in.at[1])]
+    corner_below, row_below = both(gc_out.at[1], gc_in.at[0], "d"), [message("d", C.at[second, pl.ds(192, 64)], gr_in.at[0])]
     out_edge = both(g0_out, g0_in)
     out_rest = both(g1_out, g1_in)
 
     local[0].wait()
-    for k in range(2):
-        pack(side_out.at[k], E[0, 64 + 128 * k : 128 + 128 * k], E[0, 128 + 128 * k : 192 + 128 * k])
+    pack(side_out, E[0, 128:192], E[0, 192:256])
     pack(corner_out.at[0], E[0, 256:288], E[0, 288:320])
     pack(corner_out.at[1], E[0, 64:96], E[0, 96:128])
-    def heard(way):
-        return jnp.logical_and(there(way), jnp.logical_not(opens)) if way[0] == "u" else there(way)
-
-    pl.semaphore_wait(barrier, sum(heard(way).astype(jnp.int32) for way in ways))
-    for k, way in enumerate(("d", "dl", "dr")):
-        @pl.when(jnp.logical_and(there(way), closes))
-        def _():
-            pl.semaphore_signal(ready.at[k], inc=1, device_id=device(way), device_id_type=MESH)
-
-    start(side[0] + side[1] + to_below)
-    start(to_above, jnp.logical_not(opens))
+    pl.semaphore_wait(barrier, sum(cond.astype(jnp.int32) for cond in hears.values()))
+    word(ready.at[0], "d", jnp.logical_and(closes, near["d"]))
+    word(ready.at[1], "d", inner_down)
+    word(ready.at[2], "u", inner_up)
+    start(to_below, closes)
+    start(side)
+    start(edges[0], upper)
+    start(edges[1], lower)
+    start(to_below[2:], jnp.logical_not(closes))
+    start(to_above[2:], jnp.logical_not(opens))
+    start(edges[1], upper)
+    start(edges[0], lower)
 
     local[3].wait()
     split_first(tab_v, t)
     local[1].wait()
     local[2].wait()
     kernel_spectra(t, k_v, c_s.at[0], H)
+    hear(ready.at[2], inner_down)
+    start(to_below[:2], jnp.logical_not(closes))
+    hear(ready.at[1], inner_up)
+    start(to_above[:2], jnp.logical_not(opens))
     local[4].wait()
     split_second(tab_v, t)
     local[5].wait()
@@ -292,6 +318,7 @@
 
     def spectrum(n, b):
         unpack(corner_in.at[b], pl.multiple_of(320 * b, 64))
+        unpack(edge_in.at[b], pl.multiple_of(64 + 192 * b, 64))
         span = pl.ds(pl.multiple_of(128 * b, 128), 256)
         mask_spectrum(t, lanes(E[0, span], E[1, span]), M.at[n])
 
@@ -309,19 +336,13 @@
         start_row = outer(b)
         pack(gc_out.at[b], S[n, pl.ds(start_row, 32)], S[n, pl.ds(start_row + 32, 32)], 1)
 
-    for odd in (1, 0):
-        for (copy, way), k in zip(to_above, (2, 1, 0)):
-            column = c + sum(shift[w][1] for w in way)
-            @pl.when(jnp.logical_and(jnp.logical_and(there(way), opens), lax.rem(lax.div(column, 2), 2) == odd))
-            def _(copy=copy, k=k):
-                pl.semaphore_wait(ready.at[k], 1)
-                copy.start()
-
-    arrive(side[0] + side[1])
-    arrive(to_below, upper)
-    arrive(to_above, lower)
-    unpack(side_in.at[0], 64)
-    unpack(side_in.at[1], 192)
+    hear(ready.at[0], jnp.logical_and(opens, near["u"]))
+    start(to_above, opens)
+
+    arrive(side)
+    arrive(edges[0] + to_below, upper)
+    arrive(edges[1] + to_above, lower)
+    unpack(side_in, 128)
     spectrum(0, first)
     for j in range(8):
         field_rows(t, H, M.at[0], d_s.at[0], z_s.at[0], j)
@@ -337,12 +358,14 @@
     pack_outer(0, first)
     edge_row = edge(first)
     pack(g0_out, S[0, pl.ds(edge_row, 32)], S[0, pl.ds(edge_row + 32, 32)], 1)
+    start(corner_above, upper)
+    start(corner_below, lower)
+    start(out_edge)
     C[0] = final_columns(t, zz, OWN)
-    start(out_above, upper)
-    start(out_below, lower)
-    start(out_edge)
-    arrive(to_below, lower)
-    arrive(to_above, upper)
+    start(row_above, upper)
+    start(row_below, lower)
+    arrive(edges[0] + to_below, lower)
+    arrive(edges[1] + to_above, upper)
     spectrum(1, second)
     for j in range(8):
         field_rows(t, H, M.at[1], d_s.at[1], z_s.at[1], j)
@@ -360,55 +383,73 @@
     pack_outer(1, second)
     middle = S[first, 128:256] + S[second, 0:128]
     pack(g1_out, middle[:96], rows(middle[96:], S[1, pl.ds(edge(second), 64)]), 1)
+    start(out_rest)
+    start(corner_above, lower)
+    start(corner_below, upper)
     C[1] = final_columns(t, zz, OWN)
-    start(out_rest)
-    start(out_above, lower)
-    start(out_below, upper)
+    start(row_above, lower)
+    start(row_below, upper)
     grad_v[:64] = C[first, 64:128]
     grad_v[64:192] = C[first, 128:256] + C[second, 0:128]
     grad_v[192:] = C[second, 128:192]
 
-    def gain(ref):
-        low, from_right, from_left = is_low(ref.shape[1]), ref[0], ref[1]
-        return rows(jnp.where(low, from_left, from_right), swap(jnp.where(low, from_right, from_left)))
-
-    arrive(out_edge + out_rest + out_above + out_below)
-    rest = gain(g1_in)
-    grad_v[64:192] += rest[:128]
-    grad_v[pl.ds(pl.multiple_of(192 * second, 64), 64)] += rest[128:]
-    grad_v[pl.ds(pl.multiple_of(192 * first, 64), 64)] += gain(g0_in)
-    grad_v[:64] += gain(gc_in.at[0]) + gr_in[0]
-    grad_v[192:] += gain(gc_in.at[1]) + gr_in[1]
-    gradient_out = pltpu.make_async_copy(grad_v, gradient, local_sem.at[7])
-    gradient_out.start()
+    partial_out = pltpu.make_async_copy(grad_v, partial, local_sem.at[7])
+    partial_out.start()
+    arrive(out_edge + out_rest + corner_above + corner_below + row_above + row_below)
     for copy, way in sent:
         @pl.when(there(way))
         def _():
             copy.wait_send()
     aerial_out.wait()
-    gradient_out.wait()
-
-
-def hand_over(first, second, first_out, second_out, buf, sem):
-    ins = [pltpu.make_async_copy(src, buf.at[n], sem.at[n]) for n, src in enumerate((first, second))]
-    outs = [pltpu.make_async_copy(buf.at[n], dst, sem.at[2 + n]) for n, dst in enumerate((first_out, second_out))]
+    partial_out.wait()
+
+
+def add_up(aerial, partial, g0, g1, gc, gr, aerial_out, gradient_out,
+           aerial_v, grad_v, g0_v, g1_v, gc_v, gr_v, sem):
+    ins = [pltpu.make_async_copy(src, dst, sem.at[n]) for n, (src, dst) in enumerate((
+        (aerial, aerial_v), (partial, grad_v), (g0, g0_v), (g1, g1_v), (gc, gc_v), (gr, gr_v)))]
     for copy in ins:
         copy.start()
-    for copy, out in zip(ins, outs):
+    r, c = lax.axis_index("row"), lax.axis_index("col")
+    nr, nc = lax.axis_size("row"), lax.axis_size("col")
+    up, down, left, right = r > 0, r < nr - 1, c > 0, c < nc - 1
+    first = lower_first(r).astype(jnp.int32)
+
+    def gain(ref, cond=None):
+        from_right, from_left = ref[0], ref[1]
+        here_right = right if cond is None else jnp.logical_and(right, cond)
+        here_left = left if cond is None else jnp.logical_and(left, cond)
+        from_right = jnp.where(here_right, from_right, 0.0)
+        from_left = jnp.where(here_left, from_left, 0.0)
+        low = lax.broadcasted_iota(jnp.int32, from_left.shape, 1) < 64
+        return rows(jnp.where(low, from_left, from_right), swap(jnp.where(low, from_right, from_left)))
+
+    ins[0].wait()
+    aerial_copy = pltpu.make_async_copy(aerial_v, aerial_out, sem.at[6])
+    aerial_copy.start()
+    for copy in ins[1:]:
         copy.wait()
-        out.start()
-    for out in outs:
-        out.wait()
+    rest = gain(g1_v)
+    grad_v[64:192] += rest[:128]
+    grad_v[pl.ds(pl.multiple_of(192 * (1 - first), 64), 64)] += rest[128:]
+    grad_v[pl.ds(pl.multiple_of(192 * first, 64), 64)] += gain(g0_v)
+    grad_v[:64] += gain(gc_v.at[0], up) + jnp.where(up, gr_v[0], 0.0)
+    grad_v[192:] += gain(gc_v.at[1], down) + jnp.where(down, gr_v[1], 0.0)
+    gradient_copy = pltpu.make_async_copy(grad_v, gradient_out, sem.at[7])
+    gradient_copy.start()
+    aerial_copy.wait()
+    gradient_copy.wait()
 
 
 def local(mask_field, target, kernel_real, kernel_imag):
     V, HBM = pltpu.VMEM, pltpu.HBM
     tile = jax.ShapeDtypeStruct(mask_field.shape, F32)
+    landing = tuple(jax.ShapeDtypeStruct(shape, F32) for shape in ((2, 32, 128), (2, 96, 128), (2, 2, 32, 128), (2, 64, 128)))
     results = pl.pallas_call(
         kernel,
-        out_shape=(tile, tile),
+        out_shape=(tile, tile) + landing,
         in_specs=[pl.BlockSpec(memory_space=HBM)] * 5,
-        out_specs=[pl.BlockSpec(memory_space=HBM)] * 2,
+        out_specs=[pl.BlockSpec(memory_space=HBM)] * 6,
         scratch_shapes=[
             V((2, 384, 128), F32),
             V((256, 128), jnp.int32),
@@ -426,32 +467,29 @@
             V((2, 256, 128), F32),
             V((256, 128), F32),
             V((256, 128), F32),
-            V((2, 2, 64, 128), F32),
-            V((2, 2, 64, 128), F32),
+            V((2, 64, 128), F32),
+            V((2, 64, 128), F32),
+            V((2, 2, 32, 128), F32),
             V((2, 2, 32, 128), F32),
             V((2, 2, 32, 128), F32),
             V((2, 32, 128), F32),
-            V((2, 32, 128), F32),
-            V((2, 96, 128), F32),
             V((2, 96, 128), F32),
             V((2, 2, 32, 128), F32),
-            V((2, 2, 32, 128), F32),
-            V((2, 64, 128), F32),
             pltpu.SemaphoreType.DMA((8,)),
-            pltpu.SemaphoreType.DMA((20,)),
-            pltpu.SemaphoreType.DMA((20,)),
+            pltpu.SemaphoreType.DMA((22,)),
+            pltpu.SemaphoreType.DMA((22,)),
             pltpu.SemaphoreType.REGULAR((3,)),
         ] + [V(shape, BF16) for shape in SPLITS.values()],
         compiler_params=pltpu.CompilerParams(vmem_limit_bytes=60 * 2**20, collective_id=0, has_side_effects=True),
         name="litho",
     )(mask_field, target, kernel_real, kernel_imag, jnp.asarray(TABLE))
     return pl.pallas_call(
-        hand_over,
+        add_up,
         out_shape=(tile, tile),
-        in_specs=[pl.BlockSpec(memory_space=HBM)] * 2,
+        in_specs=[pl.BlockSpec(memory_space=HBM)] * 6,
         out_specs=[pl.BlockSpec(memory_space=HBM)] * 2,
-        scratch_shapes=[V((2, 256, 128), F32), pltpu.SemaphoreType.DMA((4,))],
-        name="hand_over",
+        scratch_shapes=[V(tile.shape, F32)] * 2 + [V(x.shape, F32) for x in landing] + [pltpu.SemaphoreType.DMA((8,))],
+        name="add_up",
     )(*results)
 
 

time: 36.4 us -> 35.5 us (0.975)
  the two profiles are of different devices: /device:TPU:12 before, /device:TPU:13 now
where the time goes in v2:
time: 35.5 us; the launch traced here: 35.3 us
  Pallas kernels  34.7 us (98%)
  between operations  0.64 us (2%)
    pallas_call x1, Pallas kernels, local(): pl.pallas_call(kernel, out_shape=(tile, tile) + landing, in_specs=[pl.Blo...  32.8 us
    pallas_call x1, Pallas kernels, local(): pl.pallas_call(add_up, out_shape=(tile, tile), in_specs=[pl.BlockSpec(mem...  1.9 us

profile of v2, /device:TPU:13, one launch (start us, length us, event | category | flops | bytes accessed | tf_op | source)
XLA Modules:
  0.0 35.3 jit_solution(10032687579231287684)
XLA Ops:
  0.6 32.8 %litho.1 = (f32[256,128]{1,0:T(8,128)}, f32[256,128]{1,0:T(8,128)}, f32[2,32,128]{2,1,0:T(8,128)}, f32[2,96,128]{2,1,0:T(8,128)}, f32[2,2,32,128]{3,2,1,0:T(8,128)}, /*index=5*/f32[2,64,128]{2,1,0:T(8,128)}) custom-call(f32[256,128]{1,0:T(8,128)} %mask.1, s32[256,128]{1,0:T(8,128)} %target.1, f32[4,128,128]{2,1,0:T(8,128)} %kr.1, f32[4,128,128]{2,1,0:T(8,128)} %ki.1, ...), custom_call_target="tpu_custom_call" | custom-call | tf_op jit(solution)/shard_map/litho/pallas_call | solution.py:448
  33.4 1.9 %add_up.1 = (f32[256,128]{1,0:T(8,128)}, f32[256,128]{1,0:T(8,128)}) custom-call(f32[256,128]{1,0:T(8,128)} %get-tuple-element.8.aerial, f32[256,128]{1,0:T(8,128)} %get-tuple-element.9.partial, f32[2,32,128]{2,1,0:T(8,128)} %get-tuple-element.10.g0, f32[2,96,128]{2,1,0:T(8,128)} %get-tuple-element.11.g1, f32[2,2,32,128]{3,2,1,0:T(8,128)} %get-tuple-element.12.gc, ...), custom_call_target="tpu_custom_call" | custom-call | tf_op jit(solution)/shard_map/add_up/pallas_call | solution.py:486

commit v3 on v2

--- a/solution.py
+++ b/solution.py
@@ -189,16 +189,21 @@
         local.append(pltpu.make_async_copy(src, dst, local_sem.at[n]))
         local[-1].start()
 
-    ways = ("l", "r", "u", "d", "ul", "ur", "dl", "dr")
-    barrier = pltpu.get_barrier_semaphore()
     z = lax.rem(r, 8)
     opens, closes = z == 0, z == 7
-    inner_up, inner_down = jnp.logical_and(near["u"], jnp.logical_not(opens)), jnp.logical_and(near["d"], jnp.logical_not(closes))
-    ways = ("l", "r", "u", "d", "ul", "ur", "dl", "dr")
-    tells = {"l": near["l"], "r": near["r"], "u": near["u"], "d": inner_down,
-             "ul": jnp.logical_and(opens, there("ul")), "ur": jnp.logical_and(opens, there("ur"))}
-    hears = {"l": near["l"], "r": near["r"], "u": inner_up, "d": near["d"],
-             "dl": jnp.logical_and(closes, there("dl")), "dr": jnp.logical_and(closes, there("dr"))}
+    both_hold = jnp.logical_and
+    inner_up, inner_down = both_hold(near["u"], jnp.logical_not(opens)), both_hold(near["d"], jnp.logical_not(closes))
+    outer_up, outer_down = both_hold(near["u"], opens), both_hold(near["d"], closes)
+    odd = lax.rem(lax.div(c, 2), 2) == 1
+    across = {"l": both_hold(closes, lax.rem(c, 2) == 0), "r": both_hold(closes, lax.rem(c, 2) == 1)}
+    late_here = {way: both_hold(both_hold(near[way], across[way]), odd) for way in "lr"}
+    late_there = {way: both_hold(both_hold(near[way], across[way]), jnp.logical_not(odd)) for way in "lr"}
+    tells = {"l": both_hold(near["l"], jnp.logical_not(late_here["l"])),
+             "r": both_hold(near["r"], jnp.logical_not(late_here["r"])), "u": near["u"], "d": inner_down,
+             "ul": both_hold(opens, there("ul")), "ur": both_hold(opens, there("ur"))}
+    hears = {"l": both_hold(near["l"], jnp.logical_not(late_there["l"])),
+             "r": both_hold(near["r"], jnp.logical_not(late_there["r"])), "u": inner_up, "d": near["d"],
+             "dl": both_hold(closes, there("dl")), "dr": both_hold(closes, there("dr"))}
     barrier = pltpu.get_barrier_semaphore()
     for way, cond in tells.items():
         @pl.when(cond)
@@ -225,10 +230,9 @@
     for way in "lr":
         n = 1 - place[way]
         empty(way, side_in.at[n], edge_in.at[:, n])
-        empty("u" + way, corner_in.at[0, n])
-        empty("d" + way, corner_in.at[1, n])
-    empty("u", E.at[0, pl.ds(0, 64)])
-    empty("d", E.at[0, pl.ds(320, 64)])
+        empty("u" + way, corner_in.at[n])
+    empty("u", E.at[:, pl.ds(0, 64)])
+    empty("d", E.at[:, pl.ds(320, 64)])
 
     lower = lower_first(r)
     upper = jnp.logical_not(lower)
@@ -237,24 +241,25 @@
 
     sent = []
 
-    def message(way, src, dst):
+    def message(way, src, dst, if_sent=None, if_taken=None):
         n = len(sent)
         copy = pltpu.make_async_remote_copy(src_ref=src, dst_ref=dst, send_sem=send_sem.at[n], recv_sem=recv_sem.at[n],
                                             device_id=device(way), device_id_type=MESH)
-        sent.append((copy, way))
-        return copy, way
+        go, come = there(way), there("".join(opposite[w] for w in way))
+        go = go if if_sent is None else both_hold(go, if_sent)
+        come = come if if_taken is None else both_hold(come, if_taken)
+        sent.append((copy, go, come))
+        return sent[-1]
 
     def start(messages, now=None):
-        for copy, way in messages:
-            go = there(way)
-            @pl.when(go if now is None else jnp.logical_and(go, now))
+        for copy, go, _ in messages:
+            @pl.when(go if now is None else both_hold(go, now))
             def _(copy=copy):
                 copy.start()
 
     def arrive(messages, now=None):
-        for copy, way in messages:
-            come = there("".join(opposite[w] for w in way))
-            @pl.when(come if now is None else jnp.logical_and(come, now))
+        for copy, _, come in messages:
+            @pl.when(come if now is None else both_hold(come, now))
             def _(copy=copy):
                 copy.wait_recv()
 
@@ -266,15 +271,18 @@
         ref[low_place] = jnp.where(low, first, second)
         ref[1 - low_place] = jnp.where(low, second, first)
 
-    def both(src, dst, toward=""):
-        return [message(toward + way, src.at[place[way]], dst.at[place[way]]) for way in "lr"]
+    def both(src, dst, toward="", **when):
+        return [message(toward + way, src.at[place[way]], dst.at[place[way]], **when) for way in "lr"]
 
     side = both(side_out, side_in)
     edges = [both(corner_out.at[1 - k], edge_in.at[k]) for k in range(2)]
-    to_below = both(corner_out.at[0], corner_in.at[0], "d") + [
-        message("d", E.at[0, pl.ds(256, 64)], E.at[0, pl.ds(0, 64)])]
-    to_above = both(corner_out.at[1], corner_in.at[1], "u") + [
-        message("u", E.at[0, pl.ds(64, 64)], E.at[0, pl.ds(320, 64)])]
+    corners = both(corner_out.at[0], corner_in, "d", if_sent=closes, if_taken=opens)
+    rows_down = [message("d", E.at[0, pl.ds(256, 64)], E.at[0, pl.ds(0, 64)])]
+    rows_up = [message("u", E.at[0, pl.ds(64, 64)], E.at[0, pl.ds(320, 64)])]
+    relay_down = [message("d", E.at[1, pl.ds(256, 64)], E.at[1, pl.ds(0, 64)], jnp.logical_not(closes), jnp.logical_not(opens))]
+    relay_up = [message("u", E.at[1, pl.ds(64, 64)], E.at[1, pl.ds(320, 64)])]
+    from_above = rows_down + relay_down + corners
+    from_below = rows_up + relay_up
     corner_above, row_above = both(gc_out.at[0], gc_in.at[1], "u"), [message("u", C.at[first, pl.ds(0, 64)], gr_in.at[1])]
     corner_below, row_below = both(gc_out.at[1], gc_in.at[0], "d"), [message("d", C.at[second, pl.ds(192, 64)], gr_in.at[0])]
     out_edge = both(g0_out, g0_in)
@@ -285,27 +293,20 @@
     pack(corner_out.at[0], E[0, 256:288], E[0, 288:320])
     pack(corner_out.at[1], E[0, 64:96], E[0, 96:128])
     pl.semaphore_wait(barrier, sum(cond.astype(jnp.int32) for cond in hears.values()))
-    word(ready.at[0], "d", jnp.logical_and(closes, near["d"]))
-    word(ready.at[1], "d", inner_down)
-    word(ready.at[2], "u", inner_up)
-    start(to_below, closes)
-    start(side)
-    start(edges[0], upper)
-    start(edges[1], lower)
-    start(to_below[2:], jnp.logical_not(closes))
-    start(to_above[2:], jnp.logical_not(opens))
-    start(edges[1], upper)
-    start(edges[0], lower)
+    word(ready.at[0], "d", outer_down)
+    for way in "lr":
+        word(ready.at[1 + place[way]], way, late_here[way])
+    start(corners + rows_down)
+    start(rows_up, jnp.logical_not(opens))
+    for group in (edges[0], edges[1], side):
+        for way in "lr":
+            start([group[place[way]]], jnp.logical_not(late_there[way]))
 
     local[3].wait()
     split_first(tab_v, t)
     local[1].wait()
     local[2].wait()
     kernel_spectra(t, k_v, c_s.at[0], H)
-    hear(ready.at[2], inner_down)
-    start(to_below[:2], jnp.logical_not(closes))
-    hear(ready.at[1], inner_up)
-    start(to_above[:2], jnp.logical_not(opens))
     local[4].wait()
     split_second(tab_v, t)
     local[5].wait()
@@ -317,8 +318,6 @@
         E[1, pl.ds(begin + n, n)] = swap(jnp.where(low, from_left, from_right))
 
     def spectrum(n, b):
-        unpack(corner_in.at[b], pl.multiple_of(320 * b, 64))
-        unpack(edge_in.at[b], pl.multiple_of(64 + 192 * b, 64))
         span = pl.ds(pl.multiple_of(128 * b, 128), 256)
         mask_spectrum(t, lanes(E[0, span], E[1, span]), M.at[n])
 
@@ -336,13 +335,21 @@
         start_row = outer(b)
         pack(gc_out.at[b], S[n, pl.ds(start_row, 32)], S[n, pl.ds(start_row + 32, 32)], 1)
 
-    hear(ready.at[0], jnp.logical_and(opens, near["u"]))
-    start(to_above, opens)
-
+    for way in "lr":
+        n = place[way]
+        hear(ready.at[2 - n], late_there[way])
+        start([edges[1][n], side[n], edges[0][n]], late_there[way])
+    arrive(edges[0] + edges[1])
+    unpack(edge_in.at[0], 64)
+    unpack(edge_in.at[1], 256)
+    start(relay_down)
+    start(relay_up, jnp.logical_not(opens))
+    hear(ready.at[0], outer_up)
+    start(rows_up + relay_up, opens)
     arrive(side)
-    arrive(edges[0] + to_below, upper)
-    arrive(edges[1] + to_above, lower)
     unpack(side_in, 128)
+    arrive(from_above, upper)
+    arrive(from_below, lower)
     spectrum(0, first)
     for j in range(8):
         field_rows(t, H, M.at[0], d_s.at[0], z_s.at[0], j)
@@ -364,8 +371,13 @@
     C[0] = final_columns(t, zz, OWN)
     start(row_above, upper)
     start(row_below, lower)
-    arrive(edges[0] + to_below, lower)
-    arrive(edges[1] + to_above, upper)
+    arrive(from_above, lower)
+    arrive(from_below, upper)
+
+    @pl.when(opens)
+    def _():
+        unpack(corner_in, 0)
+
     spectrum(1, second)
     for j in range(8):
         field_rows(t, H, M.at[1], d_s.at[1], z_s.at[1], j)
@@ -396,8 +408,8 @@
     partial_out = pltpu.make_async_copy(grad_v, partial, local_sem.at[7])
     partial_out.start()
     arrive(out_edge + out_rest + corner_above + corner_below + row_above + row_below)
-    for copy, way in sent:
-        @pl.when(there(way))
+    for copy, go, _ in sent:
+        @pl.when(go)
         def _():
             copy.wait_send()
     aerial_out.wait()
@@ -471,7 +483,7 @@
             V((2, 64, 128), F32),
             V((2, 2, 32, 128), F32),
             V((2, 2, 32, 128), F32),
-            V((2, 2, 32, 128), F32),
+            V((2, 32, 128), F32),
             V((2, 32, 128), F32),
             V((2, 96, 128), F32),
             V((2, 2, 32, 128), F32),

time: 35.5 us -> 33.2 us (0.935)
  the two profiles are of different devices: /device:TPU:13 before, /device:TPU:30 now
where the time goes in v3:
time: 33.2 us; the launch traced here: 33 us
  Pallas kernels  32.4 us (98%)
  between operations  0.64 us (2%)
    pallas_call x1, Pallas kernels, local(): pl.pallas_call(kernel, out_shape=(tile, tile) + landing, in_specs=[pl.Blo...  30.5 us
    pallas_call x1, Pallas kernels, local(): pl.pallas_call(add_up, out_shape=(tile, tile), in_specs=[pl.BlockSpec(mem...  1.9 us

profile of v3, /device:TPU:30, one launch (start us, length us, event | category | flops | bytes accessed | tf_op | source)
XLA Modules:
  0.0 33.0 jit_solution(4650746998123148604)
XLA Ops:
  0.6 30.5 %litho.1 = (f32[256,128]{1,0:T(8,128)}, f32[256,128]{1,0:T(8,128)}, f32[2,32,128]{2,1,0:T(8,128)}, f32[2,96,128]{2,1,0:T(8,128)}, f32[2,2,32,128]{3,2,1,0:T(8,128)}, /*index=5*/f32[2,64,128]{2,1,0:T(8,128)}) custom-call(f32[256,128]{1,0:T(8,128)} %mask.1, s32[256,128]{1,0:T(8,128)} %target.1, f32[4,128,128]{2,1,0:T(8,128)} %kr.1, f32[4,128,128]{2,1,0:T(8,128)} %ki.1, ...), custom_call_target="tpu_custom_call" | custom-call | tf_op jit(solution)/shard_map/litho/pallas_call | solution.py:460
  31.1 1.9 %add_up.1 = (f32[256,128]{1,0:T(8,128)}, f32[256,128]{1,0:T(8,128)}) custom-call(f32[256,128]{1,0:T(8,128)} %get-tuple-element.8.aerial, f32[256,128]{1,0:T(8,128)} %get-tuple-element.9.partial, f32[2,32,128]{2,1,0:T(8,128)} %get-tuple-element.10.g0, f32[2,96,128]{2,1,0:T(8,128)} %get-tuple-element.11.g1, f32[2,2,32,128]{3,2,1,0:T(8,128)} %get-tuple-element.12.gc, ...), custom_call_target="tpu_custom_call" | custom-call | tf_op jit(solution)/shard_map/add_up/pallas_call | solution.py:498

commit v4 on v3

--- a/solution.py
+++ b/solution.py
@@ -338,7 +338,7 @@
     for way in "lr":
         n = place[way]
         hear(ready.at[2 - n], late_there[way])
-        start([edges[1][n], side[n], edges[0][n]], late_there[way])
+        start([edges[1][n], edges[0][n], side[n]], late_there[way])
     arrive(edges[0] + edges[1])
     unpack(edge_in.at[0], 64)
     unpack(edge_in.at[1], 256)

time: 33.2 us -> 33 us (level)
  the two profiles are of different devices: /device:TPU:30 before, /device:TPU:11 now
where the time goes in v4:
time: 33 us; the launch traced here: 32.9 us
  Pallas kernels  32.2 us (98%)
  between operations  0.64 us (2%)
    pallas_call x1, Pallas kernels, local(): pl.pallas_call(kernel, out_shape=(tile, tile) + landing, in_specs=[pl.Blo...  30.3 us
    pallas_call x1, Pallas kernels, local(): pl.pallas_call(add_up, out_shape=(tile, tile), in_specs=[pl.BlockSpec(mem...  1.9 us

profile of v4, /device:TPU:11, one launch (start us, length us, event | category | flops | bytes accessed | tf_op | source)
XLA Modules:
  0.0 32.9 jit_solution(15459709072268715265)
XLA Ops:
  0.6 30.3 %litho.1 = (f32[256,128]{1,0:T(8,128)}, f32[256,128]{1,0:T(8,128)}, f32[2,32,128]{2,1,0:T(8,128)}, f32[2,96,128]{2,1,0:T(8,128)}, f32[2,2,32,128]{3,2,1,0:T(8,128)}, /*index=5*/f32[2,64,128]{2,1,0:T(8,128)}) custom-call(f32[256,128]{1,0:T(8,128)} %mask.1, s32[256,128]{1,0:T(8,128)} %target.1, f32[4,128,128]{2,1,0:T(8,128)} %kr.1, f32[4,128,128]{2,1,0:T(8,128)} %ki.1, ...), custom_call_target="tpu_custom_call" | custom-call | tf_op jit(solution)/shard_map/litho/pallas_call | solution.py:460
  31.0 1.9 %add_up.1 = (f32[256,128]{1,0:T(8,128)}, f32[256,128]{1,0:T(8,128)}) custom-call(f32[256,128]{1,0:T(8,128)} %get-tuple-element.8.aerial, f32[256,128]{1,0:T(8,128)} %get-tuple-element.9.partial, f32[2,32,128]{2,1,0:T(8,128)} %get-tuple-element.10.g0, f32[2,96,128]{2,1,0:T(8,128)} %get-tuple-element.11.g1, f32[2,2,32,128]{3,2,1,0:T(8,128)} %get-tuple-element.12.gc, ...), custom_call_target="tpu_custom_call" | custom-call | tf_op jit(solution)/shard_map/add_up/pallas_call | solution.py:498

commit v5 on v4

--- a/solution.py
+++ b/solution.py
@@ -181,13 +181,6 @@
 
     def device(way):
         return (r + sum(shift[w][0] for w in way), c + sum(shift[w][1] for w in way))
-
-    local = []
-    for n, (src, dst) in enumerate(((mask, E.at[0, pl.ds(64, 256)]), (kr, k_v.at[0]), (ki, k_v.at[1]),
-                                    (tab.at[pl.ds(0, FIRST)], tab_v.at[pl.ds(0, FIRST)]),
-                                    (tab.at[pl.ds(FIRST, 768)], tab_v.at[pl.ds(FIRST, 768)]), (target, target_v))):
-        local.append(pltpu.make_async_copy(src, dst, local_sem.at[n]))
-        local[-1].start()
 
     z = lax.rem(r, 8)
     opens, closes = z == 0, z == 7
@@ -209,6 +202,13 @@
         @pl.when(cond)
         def _():
             pl.semaphore_signal(barrier, inc=1, device_id=device(way), device_id_type=MESH)
+
+    local = []
+    for n, (src, dst) in enumerate(((mask, E.at[0, pl.ds(64, 256)]), (kr, k_v.at[0]), (ki, k_v.at[1]),
+                                    (tab.at[pl.ds(0, FIRST)], tab_v.at[pl.ds(0, FIRST)]),
+                                    (tab.at[pl.ds(FIRST, 768)], tab_v.at[pl.ds(FIRST, 768)]), (target, target_v))):
+        local.append(pltpu.make_async_copy(src, dst, local_sem.at[n]))
+        local[-1].start()
 
     def word(sem, way, cond):
         @pl.when(cond)

time: 33 us -> 33.1 us (level)
  no operation moved by 1% of the time
where the time goes in v5:
time: 33.1 us; the launch traced here: 32.9 us
  Pallas kernels  32.3 us (98%)
  between operations  0.64 us (2%)
    pallas_call x1, Pallas kernels, local(): pl.pallas_call(kernel, out_shape=(tile, tile) + landing, in_specs=[pl.Blo...  30.3 us
    pallas_call x1, Pallas kernels, local(): pl.pallas_call(add_up, out_shape=(tile, tile), in_specs=[pl.BlockSpec(mem...  1.9 us

profile of v5, /device:TPU:11, one launch (start us, length us, event | category | flops | bytes accessed | tf_op | source)
XLA Modules:
  0.0 32.9 jit_solution(3854102880206275774)
XLA Ops:
  0.6 30.3 %litho.1 = (f32[256,128]{1,0:T(8,128)}, f32[256,128]{1,0:T(8,128)}, f32[2,32,128]{2,1,0:T(8,128)}, f32[2,96,128]{2,1,0:T(8,128)}, f32[2,2,32,128]{3,2,1,0:T(8,128)}, /*index=5*/f32[2,64,128]{2,1,0:T(8,128)}) custom-call(f32[256,128]{1,0:T(8,128)} %mask.1, s32[256,128]{1,0:T(8,128)} %target.1, f32[4,128,128]{2,1,0:T(8,128)} %kr.1, f32[4,128,128]{2,1,0:T(8,128)} %ki.1, ...), custom_call_target="tpu_custom_call" | custom-call | tf_op jit(solution)/shard_map/litho/pallas_call | solution.py:460
  31.0 1.9 %add_up.1 = (f32[256,128]{1,0:T(8,128)}, f32[256,128]{1,0:T(8,128)}) custom-call(f32[256,128]{1,0:T(8,128)} %get-tuple-element.8.aerial, f32[256,128]{1,0:T(8,128)} %get-tuple-element.9.partial, f32[2,32,128]{2,1,0:T(8,128)} %get-tuple-element.10.g0, f32[2,96,128]{2,1,0:T(8,128)} %get-tuple-element.11.g1, f32[2,2,32,128]{3,2,1,0:T(8,128)} %get-tuple-element.12.gc, ...), custom_call_target="tpu_custom_call" | custom-call | tf_op jit(solution)/shard_map/add_up/pallas_call | solution.py:498
